TPU v7x, 32 devices: a whole 2x2x4 slice. The times are simulated.
32 devices in a mesh: rows: 8 (over z, y), grp: 4 (over x, core).
Axes of the slice: x: 2, y: 2, z: 4, core: 2. Of those that a mesh axis runs over, the one named last changes fastest.
Arguments:
- features: bfloat16 [192, 128, 2048], P('rows', None, 'grp'), may hold values from 0 to 12
- depth_weight: float32 [3, 3, 3, 2048], P(None, None, None, 'grp'), may hold values from -2 to 2
- branch_weight: bfloat16 [4, 2048, 256], P(None, 'grp'), may hold values from -0.125 to 0.125
- pool_weight: bfloat16 [2048, 256], P('grp'), may hold values from -0.125 to 0.125
- proj_weight: bfloat16 [5, 256, 256], P(None, 'grp'), may hold values from -0.15625 to 0.15625
- class_weight: bfloat16 [256, 11], replicated, may hold values from -0.375 to 0.375
- labels: int32 [192, 128], P('rows'), may hold values from 0 to 11
Outputs:
- grad_branch: float32 [4, 2048, 256], P(None, 'grp')
- grad_depth: float32 [3, 3, 3, 2048], P(None, None, None, 'grp')
- grad_pool: float32 [2048, 256], P('grp')
- grad_proj: float32 [5, 256, 256], P(None, 'grp')
- grad_class: float32 [256, 11], replicated
All inputs are finite; a program needn't handle non-finite values.
Results may differ from a plain program's by a relative error of at most 0.0056.
Values may be sent and summed in bfloat16 or wider, within the bound.
A program may use at most 128 MiB of HBM per device.

v0:
```python
import math
import jax
import jax.numpy as jnp
from jax import lax
from jax.sharding import PartitionSpec as P

RATES = (6, 12, 18)
MARGIN = 18


def padded_2(block, sides, width):
    for axis, dim in sides:
        count = lax.axis_size(axis)
        forward = [(i, i + 1) for i in range(count - 1)]
        backward = [(target, source) for source, target in forward]
        low = lax.ppermute(
            lax.slice_in_dim(block, block.shape[dim] - width, None, axis=dim), axis, forward
        )
        high = lax.ppermute(lax.slice_in_dim(block, 0, width, axis=dim), axis, backward)
        block = jnp.concatenate([low, block, high], axis=dim)
    return block


def depth_taps(padded, weights, height, width):
    outputs = []
    for index, rate in enumerate(RATES):
        total = jnp.zeros((height, width, padded.shape[2]), jnp.float32)
        for row_tap in range(3):
            for col_tap in range(3):
                row_start = MARGIN + (row_tap - 1) * rate
                col_start = MARGIN + (col_tap - 1) * rate
                total = (
                    total
                    + weights[index, row_tap, col_tap]
                    * padded[row_start : row_start + height, col_start : col_start + width]
                )
        outputs.append(total.astype(jnp.bfloat16))
    return outputs


def depth_grads(padded, backs, height, width):
    result = []
    for index, rate in enumerate(RATES):
        taps = []
        for row_tap in range(3):
            for col_tap in range(3):
                row_start = MARGIN + (row_tap - 1) * rate
                col_start = MARGIN + (col_tap - 1) * rate
                window = padded[row_start : row_start + height, col_start : col_start + width]
                taps.append(jnp.sum(backs[index] * window, axis=(0, 1)))
        result.append(jnp.stack(taps).reshape(3, 3, -1))
    return jnp.stack(result)


def class_head(mixed, class_weight, labels, total_pixels):
    f32 = jnp.float32
    classes = class_weight.shape[1]
    hidden = jnp.maximum(mixed, 0.0).astype(jnp.bfloat16)
    logits = jnp.einsum("pc,ck->kp", hidden, class_weight, preferred_element_type=f32)
    expo = jnp.exp(logits)
    soft = expo / jnp.sum(expo, axis=0, keepdims=True)
    label_row = labels.reshape(-1)
    onehot = (
        lax.broadcasted_iota(jnp.int32, (classes, label_row.shape[0]), 0) == label_row[None, :]
    ).astype(f32)
    valid = (label_row < classes).astype(f32)
    grad_logit = ((soft - onehot) * valid[None, :] / math.sqrt(total_pixels)).astype(jnp.bfloat16)
    class_part = jnp.einsum("pc,kp->ck", hidden, grad_logit, preferred_element_type=f32)
    back_hidden = jnp.einsum("ck,kp->pc", class_weight, grad_logit, preferred_element_type=f32)
    grad_mixed = (back_hidden * (mixed > 0)).astype(jnp.bfloat16)
    col_total = lax.psum(jnp.sum(grad_mixed.astype(f32), axis=0), "rows")
    return (grad_mixed, col_total, class_part)


def per_device(
    features, depth_weight, branch_weight, pool_weight, proj_weight, class_weight, labels
):
    f32 = jnp.float32
    highest = lax.Precision.HIGHEST
    height, width, local_in = features.shape
    pixels_local = height * width
    total_pixels = height * lax.axis_size("rows") * width
    halo_rows = padded_2(features, (("rows", 0),), MARGIN)
    padded = jnp.pad(halo_rows.astype(f32), ((0, 0), (MARGIN, MARGIN), (0, 0)))
    depth_out = depth_taps(padded, depth_weight, height, width)
    flat_inputs = [item.reshape(pixels_local, local_in) for item in [features] + depth_out]
    column_sum = jnp.sum(features.astype(f32), axis=(0, 1))
    pooled = lax.psum(column_sum, "rows") / total_pixels
    partial_pre = jnp.stack(
        [jnp.dot(flat_inputs[k], branch_weight[k], preferred_element_type=f32) for k in range(4)]
    )
    pool_part = jnp.dot(pooled, pool_weight.astype(f32), precision=highest)[None, None, :]
    pre, pool_pre = (
        lax.psum_scatter(partial_pre, "grp", scatter_dimension=2, tiled=True),
        lax.psum_scatter(pool_part, "grp", scatter_dimension=2, tiled=True),
    )
    pool_pre = pool_pre[0, 0]
    own_out = jnp.maximum(pre, 0.0).astype(jnp.bfloat16)
    own_pool = jnp.maximum(pool_pre, 0.0).astype(jnp.bfloat16)
    mixed_part = jnp.einsum("kpc,kcd->pd", own_out, proj_weight[:4], preferred_element_type=f32)
    mixed_part = (
        mixed_part
        + jnp.dot(own_pool.astype(f32), proj_weight[4].astype(f32), precision=highest)[None, :]
    )
    mixed = lax.psum(mixed_part, "grp")
    grad_mixed, col_total, class_part = class_head(mixed, class_weight, labels, total_pixels)
    back_pre = jnp.einsum("pd,kcd->kpc", grad_mixed, proj_weight[:4], preferred_element_type=f32)
    own_grad = (back_pre * (pre > 0)).astype(jnp.bfloat16)
    own_poolgrad = (
        jnp.dot(col_total, proj_weight[4].astype(f32).T, precision=highest) * (pool_pre > 0)
    ).astype(jnp.bfloat16)
    grad_pre, grad_poolpre = (
        lax.all_gather(own_grad, "grp", axis=2, tiled=True),
        lax.all_gather(own_poolgrad[None, None, :], "grp", axis=2, tiled=True),
    )
    grad_poolpre = grad_poolpre[0, 0]
    proj_part = jnp.einsum("kpc,pd->kcd", own_out, grad_mixed, preferred_element_type=f32)
    pool_proj = own_pool.astype(f32)[:, None] * col_total[None, :]
    branch_part = jnp.stack(
        [
            jnp.einsum("pc,pd->cd", flat_inputs[k], grad_pre[k], preferred_element_type=f32)
            for k in range(4)
        ]
    )
    backs = [
        jnp.einsum(
            "pd,cd->pc", grad_pre[k + 1], branch_weight[k + 1], preferred_element_type=f32
        ).reshape(height, width, local_in)
        for k in range(3)
    ]
    depth_part = depth_grads(padded, backs, height, width)
    grad_pool = pooled[:, None] * grad_poolpre.astype(f32)[None, :]
    grad_branch, grad_depth, proj_main, grad_class = lax.psum(
        (branch_part, depth_part, proj_part, class_part), "rows"
    )
    grad_proj = jnp.concatenate([proj_main, pool_proj[None]], axis=0)
    return (grad_branch, grad_depth, grad_pool, grad_proj, grad_class)


def solution(mesh):
    return jax.shard_map(
        per_device,
        mesh=mesh,
        in_specs=(
            P("rows", None, "grp"),
            P(None, None, None, "grp"),
            P(None, "grp", None),
            P("grp", None),
            P(None, "grp", None),
            P(),
            P("rows", None),
        ),
        out_specs=(
            P(None, "grp", None),
            P(None, None, None, "grp"),
            P("grp", None),
            P(None, "grp", None),
            P(),
        ),
        check_vma=False,
    )
```

profile of v0, /device:TPU:0, one launch (start us, length us, event | category | flops | bytes accessed | tf_op | source)
XLA Modules:
  0.0 927.9 jit_solution(12588569372178841400)
XLA Ops:
  7.2 5.2 fusion.69
  12.4 6.3 collective-permute-start
  20.4 110.5 %psum.49 = f32[512]{0:T(512)S(1)} all-reduce(f32[512]{0:T(512)S(1)} %convert_reduce_fusion), channel_id=1, replica_groups=mesh['rows'=8,'grp'=4] {'rows'}, use_global_device_ids=true, to_apply=%region_2.3 | all-reduce | flops 512 | bytes 4096 | tf_op jit(solution)/shard_map/psum | solution.py:88
  134.2 8.1 maximum_convert_fusion
  142.3 24.1 %add_convert_fusion.1 = bf16[24,128,512]{2,1,0:T(8,128)(2,1)S(1)} fusion(f32[60,128,512]{2,1,0:T(8,128)} %maximum_convert_fusion, f32[512]{0:T(512)S(1)} %bitcast.242, f32[512]{0:T(512)S(1)} %bitcast.243, f32[512]{0:T(512)S(1)} %bitcast.244, f32[512]{0:T(512)S(1)} %bitcast.245, f32[512]{0:T(512)S(1)} %bitcast.246, f32[512]{0:T(512)S(1)} %bitcast.247, ...), kind=kLoop, calls=%fused_computation.49 | loop fusion | flops 28311552 | bytes 37767168 | tf_op jit(solution)/shard_map/convert_element_type | solution.py:37
  168.5 19.2 %add_convert_fusion = bf16[24,128,512]{2,1,0:T(8,128)(2,1)S(1)} fusion(f32[60,128,512]{2,1,0:T(8,128)} %maximum_convert_fusion, f32[512]{0:T(512)S(1)} %bitcast.230, f32[512]{0:T(512)S(1)} %bitcast.231, f32[512]{0:T(512)S(1)} %bitcast.235, f32[512]{0:T(512)S(1)} %bitcast.236, f32[512]{0:T(512)S(1)} %bitcast.237, f32[512]{0:T(512)S(1)} %bitcast.238, ...), kind=kLoop, calls=%fused_computation.48 | loop fusion | flops 28311552 | bytes 37767168 | tf_op jit(solution)/shard_map/convert_element_type | solution.py:37
  189.4 3.6 convolution_bitcast_fusion.2
  193.0 24.6 %add_convert_fusion.2 = bf16[24,128,512]{2,1,0:T(8,128)(2,1)S(1)} fusion(f32[60,128,512]{2,1,0:T(8,128)} %maximum_convert_fusion, f32[512]{0:T(512)S(1)} %bitcast.233, f32[512]{0:T(512)S(1)} %bitcast.234, f32[512]{0:T(512)S(1)} %bitcast.225, f32[512]{0:T(512)S(1)} %bitcast.226, f32[512]{0:T(512)S(1)} %bitcast.227, f32[512]{0:T(512)S(1)} %bitcast.228, ...), kind=kLoop, calls=%fused_computation.50 | loop fusion | flops 28311552 | bytes 37767168 | tf_op jit(solution)/shard_map/convert_element_type | solution.py:37
  221.6 4.9 pad_maximum_fusion
  226.5 15.3 %copy.30 = f32[4,3072,256]{1,0,2:T(4,128)} copy(f32[4,3072,256]{2,1,0:T(8,128)} %pad_maximum_fusion) | data formatting | bytes 25165824 | tf_op jit(solution)/shard_map/stack | solution.py:89
  244.8 217.1 %all-reduce.12.cloned.1.call-done = f32[4,3072,256]{1,0,2:T(4,128)} async-done(((f32[4,3072,256]{1,0,2:T(4,128)}), f32[4,3072,256]{1,0,2:T(4,128)}) %all-reduce.12.cloned.1.call-update) | async-done | bytes 12582928
  465.6 3.8 fusion.1
  469.5 68.7 %all-reduce.10.cloned.1.call-done = f32[3072,256]{1,0:T(8,128)} async-done(((f32[3072,256]{1,0:T(8,128)}), f32[3072,256]{1,0:T(8,128)}) %all-reduce.10.cloned.1.call-update) | async-done | bytes 3145744 | tf_op jit(solution)/shard_map/psum | solution.py:105
  540.8 3.2 convert_reduce_fusion.1
  544.1 3.3 fusion.3
  552.7 5.0 fusion.12
  557.7 38.8 %all-gather.3.cloned.1.call-done = bf16[4,3072,256]{1,0,2:T(4,128)(2,1)} async-done(((bf16[4,3072,64]{1,0,2:T(4,128)(2,1)}), bf16[4,3072,256]{1,0,2:T(4,128)(2,1)}) %all-gather.3.cloned.1.call-update) | async-done | bytes 6291472 | tf_op jit(solution)/shard_map/all_gather | solution.py:113
  596.4 18.7 %fusion.68 = (bf16[1,3072,256]{1,0,2:T(2,128)(2,1)}, bf16[1,3072,256]{1,0,2:T(2,128)(2,1)}, bf16[1,3072,256]{1,0,2:T(2,128)(2,1)}, bf16[1,3072,256]{1,0,2:T(2,128)(2,1)}) fusion(bf16[4,3072,256]{1,0,2:T(4,128)(2,1)} %all-gather.3.cloned.1.call-done), kind=kLoop, calls=%fused_computation.133 | loop fusion | bytes 12582912 | tf_op jit(solution)/shard_map/slice | solution.py:121
  615.2 7.3 copy.48
  622.5 4.3 fusion.18
  626.8 24.8 %multiply_reduce_fusion.18 = (f32[512]{0:T(512)S(1)}, f32[512]{0:T(512)S(1)}, f32[512]{0:T(512)S(1)}, f32[512]{0:T(512)S(1)}, f32[512]{0:T(512)S(1)}, /*index=5*...) fusion(f32[60,128,512]{2,1,0:T(8,128)} %maximum_convert_fusion, ...), kind=kOutput, calls=%fused_computation.38 | convolution fusion | flops 833613312 | bytes 36456448 | tf_op jit(solution)/shard_map/pd,cd->pc/dot_general | solution.py:126
  651.6 7.3 copy.49
  658.9 4.3 fusion.21
  663.2 24.1 %multiply_reduce_fusion.9 = (f32[512]{0:T(512)S(1)}, f32[512]{0:T(512)S(1)}, f32[512]{0:T(512)S(1)}, f32[512]{0:T(512)S(1)}, f32[512]{0:T(512)S(1)}, /*index=5*/...) fusion(f32[60,128,512]{2,1,0:T(8,128)} %maximum_convert_fusion, ...), kind=kOutput, calls=%fused_computation.29 | convolution fusion | flops 833613312 | bytes 36456448 | tf_op jit(solution)/shard_map/pd,cd->pc/dot_general | solution.py:126
  687.4 7.3 copy.50
  694.7 4.2 fusion.24
  698.9 20.2 %multiply_reduce_fusion = (f32[512]{0:T(512)S(1)}, f32[512]{0:T(512)S(1)}, f32[512]{0:T(512)S(1)}, f32[512]{0:T(512)S(1)}, f32[512]{0:T(512)S(1)}, /*index=5*/f3...) fusion(f32[60,128,512]{2,1,0:T(8,128)} %maximum_convert_fusion, bf16[24,128,256]{2,1,0:T(8,128)(2,1)} %bitcast.217, ...), kind=kOutput, calls=%fused_computation.20 | convolution fusion | flops 833613312 | bytes 36456448 | tf_op jit(solution)/shard_map/pd,cd->pc/dot_general | solution.py:126
  719.2 7.3 copy.47
  726.5 3.2 fusion.15
  734.1 66.5 %all-reduce.14.cloned.1.call-done = (f32[3,3,3,512]{3,2,1,0:T(4,128)}, f32[256]{0:T(256)}, f32[256,11]{0,1:T(8,128)}) async-done(((f32[3,3,3,512]{3,2,1,0:T(4,128)}, f32[256]{0:T(256)}, f32[256,11]{0,1:T(8,128)}), (f32[3,3,3,512]{3,2,1,0:T(4,128)}, f32[256]{0:T(256)}, f32[256,11]{0,1:T(8,128)})) %all-reduce.14.cloned.1.call-update) | async-done | bytes 67600 | tf_op jit(solution)/shard_map/psum | solution.py:133
  801.8 5.6 all-reduce.1
  809.1 104.3 %all-reduce.16.cloned.1.call-done = (f32[4,512,256]{1,2,0:T(8,128)}, f32[4,64,256]{2,1,0:T(8,128)}) async-done(((f32[4,512,256]{1,2,0:T(8,128)}, f32[4,64,256]{2,1,0:T(8,128)}), (f32[4,512,256]{1,2,0:T(8,128)}, f32[4,64,256]{2,1,0:T(8,128)})) %all-reduce.16.cloned.1.call-update) | async-done | bytes 2359312 | tf_op jit(solution)/shard_map/psum | solution.py:133
  (85 shorter events, 40.8 us)
Async XLA Ops:
  7.2 123.8 %copy-start = (bf16[512,256]{1,0:T(8,128)(2,1)S(1)}, bf16[512,256]{1,0:T(8,128)(2,1)}, u32[]{:S(2)}) copy-start(bf16[512,256]{1,0:T(8,128)(2,1)} %param.10) | copy-start | bytes 786436
  7.2 12.8 %copy-start.2 = (bf16[24,128,512]{2,1,0:T(8,128)(2,1)S(1)}, bf16[24,128,512]{2,1,0:T(8,128)(2,1)}, u32[]{:S(2)}) copy-start(bf16[24,128,512]{2,1,0:T(8,128)(2,1)} %param.7) | copy-start | bytes 9437188
  7.2 125.0 %copy-start.13 = (f32[3,3,3,512]{3,2,1,0:T(4,128)S(1)}, f32[3,3,3,512]{3,2,1,0:T(4,128)}, u32[]{:S(2)}) copy-start(f32[3,3,3,512]{3,2,1,0:T(4,128)} %param.8) | copy-start | bytes 165892
  7.2 236.6 %reduce-scatter.4.cloned.1.call-start = ((), (), s32[]{:S(2)}) async-start(), calls=%async_computation.3 | async-start | bytes 163840
  12.4 121.8 %collective-permute-start = (bf16[18,128,512]{2,1,0:T(8,128)(2,1)}, bf16[18,128,512]{2,1,0:T(8,128)(2,1)}, u32[]{:S(2)}, u32[]{:S(2)}) collective-permute-start(bf16[18,128,512]{2,1,0:T(8,128)(2,1)} %get-tuple-element.56), channel_id=1, source_target_pairs={{0,4},{4,8},{8,12},{12,16},{16,20},{20,24},{24,28},{1,5},{5,9},{9,... | collective-permute-start | bytes 7077896 | tf_op jit(solution)/shard_map/ppermute | solution.py:16
  18.7 115.5 %collective-permute-start.1 = (bf16[18,128,512]{2,1,0:T(8,128)(2,1)}, bf16[18,128,512]{2,1,0:T(8,128)(2,1)}, u32[]{:S(2)}, u32[]{:S(2)}) collective-permute-start(bf16[18,128,512]{2,1,0:T(8,128)(2,1)} %get-tuple-element.57), channel_id=1, source_target_pairs={{4,0},{8,4},{12,8},{16,12},{20,16},{24,20},{28,24},{5,1},{9,5},{13... | collective-permute-start | bytes 7077896 | tf_op jit(solution)/shard_map/ppermute | solution.py:19
  132.1 329.7 %all-reduce.12.cloned.1.call-start = ((), (), s32[]{:S(2)}) async-start(), calls=%async_computation.4 | async-start | bytes 25165824
  166.3 2.1 copy-start.4
  187.7 1.7 copy-start.3
  217.6 1.6 copy-start.5
  217.6 4.0 copy-start.6
  241.8 0.7 copy-start.16
  241.8 2.8 copy-start.15
  241.9 296.4 %all-reduce.10.cloned.1.call-start = ((), (), s32[]{:S(2)}) async-start(), calls=%async_computation.1 | async-start | bytes 6291456 | tf_op jit(solution)/shard_map/psum | solution.py:105
  464.0 1.7 copy-start.7
  464.0 5.5 copy-start.12
  464.0 74.3 %copy-start.14 = (bf16[256,11]{0,1:T(8,128)(2,1)S(1)}, bf16[256,11]{0,1:T(8,128)(2,1)}, u32[]{:S(2)}) copy-start(bf16[256,11]{0,1:T(8,128)(2,1)} %param.12) | copy-start | bytes 16900
  469.4 127.0 %all-gather.3.cloned.1.call-start = ((), (), s32[]{:S(2)}) async-start(), calls=%async_computation.2 | async-start | bytes 7864320 | tf_op jit(solution)/shard_map/all_gather | solution.py:113
  538.2 5.8 copy-start.8
  544.1 3.3 copy-start.9
  549.8 250.9 %all-reduce.14.cloned.1.call-start = ((), (), s32[]{:S(2)}) async-start(), calls=%async_computation.5 | async-start | bytes 182272 | tf_op jit(solution)/shard_map/psum | solution.py:133
  622.5 4.3 copy-start.10
  658.9 4.3 copy-start.11
  726.5 194.3 %copy-start.1 = (bf16[512,256]{1,0:T(8,128)(2,1)S(1)}, bf16[512,256]{1,0:T(8,128)(2,1)}, u32[]{:S(2)}) copy-start(bf16[512,256]{1,0:T(8,128)(2,1)} %param.10) | copy-start | bytes 786436
  730.4 183.0 %all-reduce.16.cloned.1.call-start = ((), (), s32[]{:S(2)}) async-start(), calls=%async_computation.6 | async-start | bytes 4718592 | tf_op jit(solution)/shard_map/psum | solution.py:133
Sparse Core Ops, SparseCore 0:
  132.2 18.7 reduce-scatter.3
  242.0 219.8 all-reduce.11
  469.5 68.6 all-reduce.9
  549.9 46.4 all-gather.2
  730.5 70.0 all-reduce.13
  805.1 108.2 all-reduce.15
where the time goes:
time: 932 us; the launch traced here: 928 us
  waiting for transfers between devices  496 us (53%)
  matrix products  118 us (13%)
  blocking collectives  116 us (12%)
  other arithmetic  88.4 us (9%)
  local copies, waits for them, and re-layouts  85.7 us (9%)
  between operations  15.9 us (2%)
    unnamed x8, waiting for transfers between devices  217 us
    psum x2, waiting for transfers between devices, per_device(): lax.psum((branch_part, depth_part, proj_part, class_part), 'rows')  171 us
    psum x1, blocking collectives, per_device(): pooled = lax.psum(column_sum, 'rows') / total_pixels  111 us
    dot_general x3, matrix products, per_device(): jnp.einsum('pd,cd->pc', grad_pre[k + 1], branch_weight[k + 1], preferred_...  69 us
    psum x1, waiting for transfers between devices, per_device(): mixed = lax.psum(mixed_part, 'grp')  68.7 us
    convert_element_type x3, other arithmetic, depth_taps(): outputs.append(total.astype(jnp.bfloat16))  67.9 us
    unnamed x46, local copies, waits for them, and re-layouts  43.9 us
    all_gather x1, waiting for transfers between devices, per_device(): lax.all_gather(own_grad, 'grp', axis=2, tiled=True)  38.8 us
  transfers between devices with their start and end apart: 8, of which 5 were waited for; matrix products, arithmetic and copies ran while one was open for 13% of the time, Pallas kernels for 0%

commit v1 on v0

--- a/solution.py
+++ b/solution.py
@@ -102,7 +102,9 @@
         mixed_part
         + jnp.dot(own_pool.astype(f32), proj_weight[4].astype(f32), precision=highest)[None, :]
     )
-    mixed = lax.psum(mixed_part, "grp")
+    mixed = mixed_part
+    for hop in (1, 2):
+        mixed = mixed + lax.ppermute(mixed, "grp", [(dev, dev ^ hop) for dev in range(4)])
     grad_mixed, col_total, class_part = class_head(mixed, class_weight, labels, total_pixels)
     back_pre = jnp.einsum("pd,kcd->kpc", grad_mixed, proj_weight[:4], preferred_element_type=f32)
     own_grad = (back_pre * (pre > 0)).astype(jnp.bfloat16)

time: 932 us -> 932 us (level)
    ppermute x0 -> x2, waiting for transfers between devices: none -> 75.2 us  [per_device(): lax.ppermute(mixed, 'grp', [(dev, dev ^ hop) for dev in range(4)])]
    psum x1 -> x0, waiting for transfers between devices: 68.7 us -> none  [per_device(): mixed = lax.psum(mixed_part, 'grp')]
    unnamed x46 -> x48, local copies, waits for them, and re-layouts: 43.9 us -> 42.3 us
    unnamed x8 -> x7, waiting for transfers between devices: 217 us -> 217 us
  transfers between devices with their start and end apart: 8 -> 9, of which waited for: 5 -> 6; matrix products, arithmetic and copies ran while one was open for 13% -> 13% of each run, Pallas kernels for 0% -> 0%
where the time goes in v1:
time: 932 us; the launch traced here: 928 us
  waiting for transfers between devices  503 us (54%)
  blocking collectives  116 us (12%)
  matrix products  111 us (12%)
  other arithmetic  89.3 us (10%)
  local copies, waits for them, and re-layouts  84.1 us (9%)
  between operations  15.6 us (2%)
    unnamed x7, waiting for transfers between devices  217 us
    psum x2, waiting for transfers between devices, per_device(): lax.psum((branch_part, depth_part, proj_part, class_part), 'rows')  171 us
    psum x1, blocking collectives, per_device(): pooled = lax.psum(column_sum, 'rows') / total_pixels  111 us
    ppermute x2, waiting for transfers between devices, per_device(): lax.ppermute(mixed, 'grp', [(dev, dev ^ hop) for dev in range(4)])  75.2 us
    dot_general x3, matrix products, per_device(): jnp.einsum('pd,cd->pc', grad_pre[k + 1], branch_weight[k + 1], preferred_...  69 us
    convert_element_type x3, other arithmetic, depth_taps(): outputs.append(total.astype(jnp.bfloat16))  67.9 us
    unnamed x48, local copies, waits for them, and re-layouts  42.3 us
    all_gather x1, waiting for transfers between devices, per_device(): lax.all_gather(own_grad, 'grp', axis=2, tiled=True)  39.3 us
  transfers between devices with their start and end apart: 9, of which 6 were waited for; matrix products, arithmetic and copies ran while one was open for 13% of the time, Pallas kernels for 0%

profile of v1, /device:TPU:0, one launch (start us, length us, event | category | flops | bytes accessed | tf_op | source)
XLA Modules:
  0.0 927.5 jit_solution(9652420252882506472)
XLA Ops:
  7.2 5.2 fusion.69
  12.4 6.3 collective-permute-start
  20.4 110.5 %psum.42 = f32[512]{0:T(512)S(1)} all-reduce(f32[512]{0:T(512)S(1)} %convert_reduce_fusion), channel_id=1, replica_groups=mesh['rows'=8,'grp'=4] {'rows'}, use_global_device_ids=true, to_apply=%region_2.3 | all-reduce | flops 512 | bytes 4096 | tf_op jit(solution)/shard_map/psum | solution.py:88
  134.2 8.1 maximum_convert_fusion
  142.3 24.1 %add_convert_fusion.1 = bf16[24,128,512]{2,1,0:T(8,128)(2,1)S(1)} fusion(f32[60,128,512]{2,1,0:T(8,128)} %maximum_convert_fusion, f32[512]{0:T(512)S(1)} %bitcast.246, f32[512]{0:T(512)S(1)} %bitcast.247, f32[512]{0:T(512)S(1)} %bitcast.248, f32[512]{0:T(512)S(1)} %bitcast.249, f32[512]{0:T(512)S(1)} %bitcast.250, f32[512]{0:T(512)S(1)} %bitcast.251, ...), kind=kLoop, calls=%fused_computation.49 | loop fusion | flops 28311552 | bytes 37767168 | tf_op jit(solution)/shard_map/convert_element_type | solution.py:37
  168.5 19.2 %add_convert_fusion = bf16[24,128,512]{2,1,0:T(8,128)(2,1)S(1)} fusion(f32[60,128,512]{2,1,0:T(8,128)} %maximum_convert_fusion, f32[512]{0:T(512)S(1)} %bitcast.234, f32[512]{0:T(512)S(1)} %bitcast.235, f32[512]{0:T(512)S(1)} %bitcast.239, f32[512]{0:T(512)S(1)} %bitcast.240, f32[512]{0:T(512)S(1)} %bitcast.241, f32[512]{0:T(512)S(1)} %bitcast.242, ...), kind=kLoop, calls=%fused_computation.48 | loop fusion | flops 28311552 | bytes 37767168 | tf_op jit(solution)/shard_map/convert_element_type | solution.py:37
  189.4 3.6 convolution_bitcast_fusion.2
  193.0 24.6 %add_convert_fusion.2 = bf16[24,128,512]{2,1,0:T(8,128)(2,1)S(1)} fusion(f32[60,128,512]{2,1,0:T(8,128)} %maximum_convert_fusion, f32[512]{0:T(512)S(1)} %bitcast.237, f32[512]{0:T(512)S(1)} %bitcast.238, f32[512]{0:T(512)S(1)} %bitcast.229, f32[512]{0:T(512)S(1)} %bitcast.230, f32[512]{0:T(512)S(1)} %bitcast.231, f32[512]{0:T(512)S(1)} %bitcast.232, ...), kind=kLoop, calls=%fused_computation.50 | loop fusion | flops 28311552 | bytes 37767168 | tf_op jit(solution)/shard_map/convert_element_type | solution.py:37
  221.6 4.9 pad_maximum_fusion
  226.5 15.3 %copy.30 = f32[4,3072,256]{1,0,2:T(4,128)} copy(f32[4,3072,256]{2,1,0:T(8,128)} %pad_maximum_fusion) | data formatting | bytes 25165824 | tf_op jit(solution)/shard_map/stack | solution.py:89
  244.8 217.1 %all-reduce.9.cloned.1.call-done = f32[4,3072,256]{1,0,2:T(4,128)} async-done(((f32[4,3072,256]{1,0,2:T(4,128)}), f32[4,3072,256]{1,0,2:T(4,128)}) %all-reduce.9.cloned.1.call-update) | async-done | bytes 12582928
  466.2 5.6 collective-permute-done.2
  472.9 69.6 %collective-permute-done.3 = f32[3072,256]{1,0:T(8,128)S(1)} collective-permute-done((f32[3072,256]{1,0:T(8,128)S(1)}, f32[3072,256]{1,0:T(8,128)S(1)}, u32[]{:S(2)}, u32[]{:S(2)}) %collective-permute-start.3) | collective-permute-done | bytes 3145760 | tf_op jit(solution)/shard_map/ppermute | solution.py:107
  552.0 5.0 fusion.11
  557.1 39.3 %all-gather.3.cloned.1.call-done = bf16[4,3072,256]{1,0,2:T(4,128)(2,1)} async-done(((bf16[4,3072,64]{1,0,2:T(4,128)(2,1)}), bf16[4,3072,256]{1,0,2:T(4,128)(2,1)}) %all-gather.3.cloned.1.call-update) | async-done | bytes 6291472 | tf_op jit(solution)/shard_map/all_gather | solution.py:115
  596.4 18.7 %fusion.68 = (bf16[1,3072,256]{1,0,2:T(2,128)(2,1)}, bf16[1,3072,256]{1,0,2:T(2,128)(2,1)}, bf16[1,3072,256]{1,0,2:T(2,128)(2,1)}, bf16[1,3072,256]{1,0,2:T(2,128)(2,1)}) fusion(bf16[4,3072,256]{1,0,2:T(4,128)(2,1)} %all-gather.3.cloned.1.call-done), kind=kLoop, calls=%fused_computation.131 | loop fusion | bytes 12582912 | tf_op jit(solution)/shard_map/slice | solution.py:123
  615.1 7.3 copy.48
  622.5 4.3 fusion.17
  626.8 24.8 %multiply_reduce_fusion.18 = (f32[512]{0:T(512)S(1)}, f32[512]{0:T(512)S(1)}, f32[512]{0:T(512)S(1)}, f32[512]{0:T(512)S(1)}, f32[512]{0:T(512)S(1)}, /*index=5*...) fusion(f32[60,128,512]{2,1,0:T(8,128)} %maximum_convert_fusion, ...), kind=kOutput, calls=%fused_computation.38 | convolution fusion | flops 833613312 | bytes 36456448 | tf_op jit(solution)/shard_map/pd,cd->pc/dot_general | solution.py:128
  651.6 7.3 copy.49
  658.9 4.3 fusion.20
  663.2 24.1 %multiply_reduce_fusion.9 = (f32[512]{0:T(512)S(1)}, f32[512]{0:T(512)S(1)}, f32[512]{0:T(512)S(1)}, f32[512]{0:T(512)S(1)}, f32[512]{0:T(512)S(1)}, /*index=5*/...) fusion(f32[60,128,512]{2,1,0:T(8,128)} %maximum_convert_fusion, ...), kind=kOutput, calls=%fused_computation.29 | convolution fusion | flops 833613312 | bytes 36456448 | tf_op jit(solution)/shard_map/pd,cd->pc/dot_general | solution.py:128
  687.4 7.3 copy.50
  694.7 4.2 fusion.23
  698.9 20.2 %multiply_reduce_fusion = (f32[512]{0:T(512)S(1)}, f32[512]{0:T(512)S(1)}, f32[512]{0:T(512)S(1)}, f32[512]{0:T(512)S(1)}, f32[512]{0:T(512)S(1)}, /*index=5*/f3...) fusion(f32[60,128,512]{2,1,0:T(8,128)} %maximum_convert_fusion, bf16[24,128,256]{2,1,0:T(8,128)(2,1)} %bitcast.221, ...), kind=kOutput, calls=%fused_computation.20 | convolution fusion | flops 833613312 | bytes 36456448 | tf_op jit(solution)/shard_map/pd,cd->pc/dot_general | solution.py:128
  719.1 7.3 copy.47
  726.5 3.2 fusion.14
  730.4 3.0 pad_maximum_fusion.1
  734.1 66.5 %all-reduce.11.cloned.1.call-done = (f32[3,3,3,512]{3,2,1,0:T(4,128)}, f32[256]{0:T(256)}, f32[256,11]{0,1:T(8,128)}) async-done(((f32[3,3,3,512]{3,2,1,0:T(4,128)}, f32[256]{0:T(256)}, f32[256,11]{0,1:T(8,128)}), (f32[3,3,3,512]{3,2,1,0:T(4,128)}, f32[256]{0:T(256)}, f32[256,11]{0,1:T(8,128)})) %all-reduce.11.cloned.1.call-update) | async-done | bytes 67600 | tf_op jit(solution)/shard_map/psum | solution.py:135
  801.8 5.6 all-reduce.1
  809.1 104.3 %all-reduce.13.cloned.1.call-done = (f32[4,512,256]{1,2,0:T(8,128)}, f32[4,64,256]{2,1,0:T(8,128)}) async-done(((f32[4,512,256]{1,2,0:T(8,128)}, f32[4,64,256]{2,1,0:T(8,128)}), (f32[4,512,256]{1,2,0:T(8,128)}, f32[4,64,256]{2,1,0:T(8,128)})) %all-reduce.13.cloned.1.call-update) | async-done | bytes 2359312 | tf_op jit(solution)/shard_map/psum | solution.py:135
  913.3 2.9 copy.41
  (90 shorter events, 38.1 us)
Async XLA Ops:
  7.2 123.8 %copy-start = (bf16[512,256]{1,0:T(8,128)(2,1)S(1)}, bf16[512,256]{1,0:T(8,128)(2,1)}, u32[]{:S(2)}) copy-start(bf16[512,256]{1,0:T(8,128)(2,1)} %param.10) | copy-start | bytes 786436
  7.2 12.8 %copy-start.2 = (bf16[24,128,512]{2,1,0:T(8,128)(2,1)S(1)}, bf16[24,128,512]{2,1,0:T(8,128)(2,1)}, u32[]{:S(2)}) copy-start(bf16[24,128,512]{2,1,0:T(8,128)(2,1)} %param.7) | copy-start | bytes 9437188
  7.2 125.0 %copy-start.13 = (f32[3,3,3,512]{3,2,1,0:T(4,128)S(1)}, f32[3,3,3,512]{3,2,1,0:T(4,128)}, u32[]{:S(2)}) copy-start(f32[3,3,3,512]{3,2,1,0:T(4,128)} %param.8) | copy-start | bytes 165892
  7.2 236.6 %reduce-scatter.4.cloned.1.call-start = ((), (), s32[]{:S(2)}) async-start(), calls=%async_computation.2 | async-start | bytes 163840
  12.4 121.8 %collective-permute-start = (bf16[18,128,512]{2,1,0:T(8,128)(2,1)}, bf16[18,128,512]{2,1,0:T(8,128)(2,1)}, u32[]{:S(2)}, u32[]{:S(2)}) collective-permute-start(bf16[18,128,512]{2,1,0:T(8,128)(2,1)} %get-tuple-element.56), channel_id=1, source_target_pairs={{0,4},{4,8},{8,12},{12,16},{16,20},{20,24},{24,28},{1,5},{5,9},{9,... | collective-permute-start | bytes 7077896 | tf_op jit(solution)/shard_map/ppermute | solution.py:16
  18.7 115.5 %collective-permute-start.1 = (bf16[18,128,512]{2,1,0:T(8,128)(2,1)}, bf16[18,128,512]{2,1,0:T(8,128)(2,1)}, u32[]{:S(2)}, u32[]{:S(2)}) collective-permute-start(bf16[18,128,512]{2,1,0:T(8,128)(2,1)} %get-tuple-element.57), channel_id=1, source_target_pairs={{4,0},{8,4},{12,8},{16,12},{20,16},{24,20},{28,24},{5,1},{9,5},{13... | collective-permute-start | bytes 7077896 | tf_op jit(solution)/shard_map/ppermute | solution.py:19
  132.1 329.7 %all-reduce.9.cloned.1.call-start = ((), (), s32[]{:S(2)}) async-start(), calls=%async_computation.3 | async-start | bytes 25165824
  166.3 2.1 copy-start.4
  187.7 1.7 copy-start.3
  217.6 1.6 copy-start.5
  217.6 4.0 copy-start.6
  241.8 0.7 copy-start.17
  241.8 2.8 copy-start.15
  241.9 354.5 %all-gather.3.cloned.1.call-start = ((), (), s32[]{:S(2)}) async-start(), calls=%async_computation.1 | async-start | bytes 7864320 | tf_op jit(solution)/shard_map/all_gather | solution.py:115
  464.0 81.0 %copy-start.8 = (f32[4,3072,64]{1,0,2:T(4,128)}, f32[4,3072,64]{1,0,2:T(4,128)S(1)}, u32[]{:S(2)}) copy-start(f32[4,3072,64]{1,0,2:T(4,128)S(1)} %constant_dynamic-slice_fusion) | copy-start | bytes 9437188
  466.1 6.8 copy-start.12
  466.1 5.7 collective-permute-start.2
  472.3 70.7 %copy-start.14 = (bf16[256,11]{0,1:T(8,128)(2,1)S(1)}, bf16[256,11]{0,1:T(8,128)(2,1)}, u32[]{:S(2)}) copy-start(bf16[256,11]{0,1:T(8,128)(2,1)} %param.12) | copy-start | bytes 16900
  472.3 70.2 %collective-permute-start.3 = (f32[3072,256]{1,0:T(8,128)S(1)}, f32[3072,256]{1,0:T(8,128)S(1)}, u32[]{:S(2)}, u32[]{:S(2)}) collective-permute-start(f32[3072,256]{1,0:T(8,128)S(1)} %add.130), channel_id=1, source_target_pairs={{0,2},{1,3},{2,0},{3,1},{4,6},{5,7},{6,4},{7,5},{8,10},{9,11},{10,... | collective-permute-start | bytes 9437192 | tf_op jit(solution)/shard_map/ppermute | solution.py:107
  543.0 4.3 copy-start.7
  543.0 1.9 copy-start.16
  544.9 2.3 copy-start.9
  549.7 251.0 %all-reduce.11.cloned.1.call-start = ((), (), s32[]{:S(2)}) async-start(), calls=%async_computation.4 | async-start | bytes 182272 | tf_op jit(solution)/shard_map/psum | solution.py:135
  622.5 4.3 copy-start.10
  658.9 4.3 copy-start.11
  726.5 194.3 %copy-start.1 = (bf16[512,256]{1,0:T(8,128)(2,1)S(1)}, bf16[512,256]{1,0:T(8,128)(2,1)}, u32[]{:S(2)}) copy-start(bf16[512,256]{1,0:T(8,128)(2,1)} %param.10) | copy-start | bytes 786436
  730.4 183.0 %all-reduce.13.cloned.1.call-start = ((), (), s32[]{:S(2)}) async-start(), calls=%async_computation.5 | async-start | bytes 4718592 | tf_op jit(solution)/shard_map/psum | solution.py:135
Sparse Core Ops, SparseCore 0:
  132.2 18.7 reduce-scatter.3
  242.0 219.8 all-reduce.8
  549.8 46.5 all-gather.2
  730.5 70.0 all-reduce.10
  805.1 108.2 all-reduce.12
